TPU v7x, 32 devices: a whole 2x2x4 slice. The times are simulated.
32 devices in a mesh: space: 8 (over z, core), filt: 4 (over y, x).
Axes of the slice: x: 2, y: 2, z: 4, core: 2. Of those that a mesh axis runs over, the one named last changes fastest.
Arguments:
- volume: bfloat16 [4, 16, 256, 512], P(None, 'space', 'filt'), may hold values from -6 to 6
- first_kernel: bfloat16 [32, 4, 3, 3, 3], replicated, may hold values from -0.625 to 0.625
- second_kernel: bfloat16 [64, 32, 2, 2, 2], replicated, may hold values from -0.375 to 0.375
- upstream: bfloat16 [64, 8, 32768], P('filt', None, 'space'), may hold values from -0.03125 to 0.03125
Outputs:
- pooled: bfloat16 [64, 8, 32768], P('filt', None, 'space')
- grad_first: float32 [32, 4, 3, 3, 3], P('filt')
- grad_second: float32 [64, 32, 2, 2, 2], P(None, 'filt')
All inputs are finite; a program needn't handle non-finite values.
Results may differ from a plain program's by a relative error of at most 0.013.
Values may be sent and summed in bfloat16 or wider, within the bound.
A program may use at most 256 MiB of HBM per device.

v0:
```python
import jax
import jax.numpy as jnp
from jax import lax
from jax.sharding import PartitionSpec as P

SLOPE = 0.3
NUMBERS = ("NCDHW", "OIDHW", "NCDHW")


def with_halo(cells, sides, width):
    for axis, dim in sides:
        count = lax.axis_size(axis)
        ends = count - 1
        head = lax.slice_in_dim(cells, 0, width, axis=dim)
        tail = lax.slice_in_dim(cells, cells.shape[dim] - width, cells.shape[dim], axis=dim)
        cells = jnp.concatenate(
            [
                lax.ppermute(tail, axis, [(i, (i + 1) % count) for i in range(ends)]),
                cells,
                lax.ppermute(head, axis, [((i + 1) % count, i) for i in range(ends)]),
            ],
            axis=dim,
        )
    return cells


def convolve(left_operand, right_operand, strides, padding, lhs_dilation=None, rhs_dilation=None):
    return lax.conv_general_dilated(
        left_operand,
        right_operand,
        strides,
        padding,
        lhs_dilation=lhs_dilation,
        rhs_dilation=rhs_dilation,
        dimension_numbers=NUMBERS,
        preferred_element_type=jnp.float32,
    )


def first_layer(framed, kernel):
    first_out = convolve(framed[None], kernel, (1, 1, 1), "VALID")[0]
    return jnp.where(first_out > 0, first_out, SLOPE * first_out).astype(jnp.bfloat16)


def second_layer(active, kernel):
    return convolve(active[None], kernel, (2, 2, 2), "VALID")[0]


def spread_back(gradient, kernel):
    flipped = jnp.flip(kernel, (2, 3, 4)).transpose(1, 0, 2, 3, 4)
    return convolve(
        gradient[None], flipped, (1, 1, 1), ((1, 1), (1, 1), (1, 1)), lhs_dilation=(2, 2, 2)
    )[0]


def kernel_grads(framed, active, back_flow, gradient):
    slopes = jnp.where(active > 0, 1.0, SLOPE).astype(jnp.float32)
    steered = (back_flow * slopes).astype(jnp.bfloat16)
    second_term = convolve(
        active[:, None], gradient[:, None], (1, 1, 1), "VALID", rhs_dilation=(2, 2, 2)
    ).transpose(1, 0, 2, 3, 4)
    first_term = convolve(framed[:, None], steered[:, None], (1, 1, 1), "VALID").transpose(
        1, 0, 2, 3, 4
    )
    return (first_term, second_term)


def shards(volume, first_kernel, second_kernel, upstream):
    groups = lax.axis_size("filt")
    group_size = first_kernel.shape[0] // groups
    offset = lax.axis_index("filt") * group_size
    half_cols = volume.shape[3] // 2
    band_rows = upstream.shape[2] // half_cols
    grid_up = upstream.reshape(upstream.shape[0], upstream.shape[1], band_rows, half_cols)
    faced = with_halo(volume, (("space", 1), ("filt", 2)), 1)
    framed = jnp.pad(faced, ((0, 0), (0, 0), (0, 0), (1, 1)))
    active = first_layer(framed, first_kernel)
    pooled_local = second_layer(active, second_kernel).astype(jnp.bfloat16)
    moved = lax.all_to_all(
        lax.all_to_all(pooled_local, "filt", split_axis=0, concat_axis=2, tiled=True),
        "space",
        split_axis=2,
        concat_axis=1,
        tiled=True,
    )
    pooled = moved.reshape(moved.shape[0], moved.shape[1], moved.shape[2] * moved.shape[3])
    local_up = lax.all_to_all(
        lax.all_to_all(grid_up, "space", split_axis=1, concat_axis=2, tiled=True),
        "filt",
        split_axis=2,
        concat_axis=0,
        tiled=True,
    )
    back_flow = spread_back(local_up, second_kernel)
    first_term, second_term = kernel_grads(framed, active, back_flow, local_up)
    full_first, full_second = lax.psum((first_term, second_term), ("space", "filt"))
    grad_first = lax.dynamic_slice_in_dim(full_first, offset, group_size, 0)
    grad_second = lax.dynamic_slice_in_dim(full_second, offset, group_size, 1)
    return (pooled, grad_first, grad_second)


def solution(mesh):
    in_specs = (P(None, "space", "filt", None), P(), P(), P("filt", None, "space"))
    out_specs = (
        P("filt", None, "space"),
        P("filt", None, None, None, None),
        P(None, "filt", None, None, None),
    )
    return jax.shard_map(shards, mesh=mesh, in_specs=in_specs, out_specs=out_specs, check_vma=False)
```

profile of v0, /device:TPU:9, one launch (start us, length us, event | category | flops | bytes accessed | tf_op | source)
XLA Modules:
  0.0 1186.4 jit_solution(4181858897372337962)
XLA Ops:
  38.6 15.8 %copy.121 = bf16[4,4,66,1,8,65]{4,0,5,2,1,3:T(4,128)(2,1)} copy(bf16[4,4,66,1,8,65]{5,4,2,1,0,3:T(8,128)(2,1)S(1)} %reshape.134) | data formatting | bytes 2196480 | tf_op jit(solution)/shard_map/conv_general_dilated | solution.py:28
  55.9 25.5 %fusion.5.clone.4 = bf16[4,4,66,8,67]{3,0,4,2,1:T(4,128)(2,1)} fusion(bf16[4,4,66,1,7,2]{4,0,5,2,1,3:T(4,128)(2,1)S(1)} %slice.24, bf16[4,4,66,1,8,65]{4,0,5,2,1,3:T(4,128)(2,1)} %copy.121), kind=kLoop, calls=%fused_computation.9.clone.clone.clone.clone.1 | loop fusion | flops 3396096 | bytes 2259840 | tf_op jit(solution)/shard_map/convert_element_type | solution.py:42
  81.4 84.6 %fusion.13 = (bf16[2,64,8,65,32]{4,2,3,1,0:T(8,128)(2,1)}, f32[2,64,8,65,32]{4,2,3,1,0:T(8,128)}) fusion(pred[8,65]{0,1:T(8,128)(4,1)S(1)} %copy-done.6, bf16[32,4,3,3,3]{0,1,4,3,2:T(4,128)(2,1)S(1)} %copy-done.5, bf16[4,4,66,8,67]{3,0,4,2,1:T(4,128)(2,1)} %fusion.5.clone.4), kind=kOutput, calls=%fused_computation.17 | convolution fusion | flops 472842240 | bytes 13918984 | tf_op jit(solution)/shard_map/conv_general_dilated | solution.py:28
  166.0 20.7 %copy.122 = bf16[2,64,8,65,32]{3,2,4,1,0:T(8,128)(2,1)} copy(bf16[2,64,8,65,32]{4,2,3,1,0:T(8,128)(2,1)} %get-tuple-element.29) | data formatting | bytes 8519680 | tf_op jit(solution)/shard_map/convert_element_type | solution.py:42
  186.7 13.1 %reshape.105 = bf16[2,64,1,520,32]{3,4,1,0,2:T(8,128)(2,1)} reshape(bf16[2,64,8,65,32]{3,2,4,1,0:T(8,128)(2,1)} %copy.122) | data formatting | bytes 8519680 | tf_op jit(solution)/shard_map/convert_element_type | solution.py:42
  199.8 4.9 slice.25
  204.7 11.2 reshape.108
  215.9 18.7 %copy.124 = bf16[2,64,1,8,64,32]{5,3,4,1,0,2:T(8,128)(2,1)} copy(bf16[2,64,1,8,64,32]{4,3,5,1,0,2:T(8,128)(2,1)} %reshape.108) | data formatting | bytes 8388608 | tf_op jit(solution)/shard_map/convert_element_type | solution.py:42
  235.6 10.3 fusion.24
  256.0 11.8 all-to-all-done
  271.3 28.5 %copy.141 = f32[2,64,8,65,32]{3,2,4,1,0:T(8,128)} copy(f32[2,64,8,65,32]{4,2,3,1,0:T(8,128)} %get-tuple-element.30) | data formatting | bytes 17039360 | tf_op jit(solution)/shard_map/conv_general_dilated | solution.py:28
  299.8 16.6 %reshape.102 = f32[2,64,1,520,32]{3,4,1,0,2:T(8,128)} reshape(f32[2,64,8,65,32]{3,2,4,1,0:T(8,128)} %copy.141) | data formatting | bytes 17039360 | tf_op jit(solution)/shard_map/conv_general_dilated | solution.py:28
  316.4 94.3 %copy.142 = bf16[4,1,4,66,514]{0,1,4,3,2:T(2,128)(2,1)} copy(bf16[4,1,4,66,514]{4,3,2,0,1:T(8,128)(2,1)S(1)} %copy-done.2) | data formatting | bytes 2171136 | tf_op jit(solution)/shard_map/broadcast_in_dim | solution.py:62
  413.7 5.4 all-to-all-start.1
  426.1 5.0 copy.146
  431.1 12.9 %broadcast_select_fusion = f32[2,64,8,66,32]{4,2,3,1,0:T(8,128)} fusion(pred[8,66]{0,1:T(8,128)(4,1)S(1)} %copy-done.4, bf16[64,1,32,8,33]{0,2,4,3,1:T(8,128)(2,1)S(1)} %bitcast.83, bf16[64,32,2,2,2]{0,4,3,2,1:T(2,128)(2,1)S(1)} %copy-done), kind=kOutput, calls=%fused_computation.13 | convolution fusion | flops 278986752 | bytes 9765392 | tf_op jit(solution)/shard_map/conv_general_dilated | solution.py:28
  444.0 28.6 %copy.140 = f32[2,64,8,66,32]{3,2,4,1,0:T(8,128)} copy(f32[2,64,8,66,32]{4,2,3,1,0:T(8,128)} %broadcast_select_fusion) | data formatting | bytes 17301504 | tf_op jit(solution)/shard_map/conv_general_dilated | solution.py:28
  472.6 16.5 %reshape.118 = f32[2,64,1,528,32]{3,4,1,0,2:T(8,128)} reshape(f32[2,64,8,66,32]{3,2,4,1,0:T(8,128)} %copy.140) | data formatting | bytes 17301504 | tf_op jit(solution)/shard_map/conv_general_dilated | solution.py:28
  489.1 9.3 fusion.21
  498.4 61.6 %copy.143 = bf16[32,1,2,64,512]{0,1,4,3,2:T(2,128)(2,1)} copy(bf16[32,1,2,64,512]{4,0,3,2,1:T(8,128)(2,1)} %get-tuple-element.21) | data formatting | bytes 8388608 | tf_op jit(solution)/shard_map/convert_element_type | solution.py:58
  560.0 61.3 %copy.145 = bf16[32,1,2,64,512]{0,1,4,3,2:T(2,128)(2,1)} copy(bf16[32,1,2,64,512]{4,0,3,2,1:T(8,128)(2,1)} %get-tuple-element.22) | data formatting | bytes 8388608 | tf_op jit(solution)/shard_map/convert_element_type | solution.py:42
  621.3 59.5 %fusion.46 = f32[64,32,2,2,2]{0,1,4,3,2:T(8,128)} fusion(bf16[32,1,2,64,512]{0,1,4,3,2:T(2,128)(2,1)} %copy.145, bf16[64,1,1,32,256]{0,1,4,3,2:T(2,128)(2,1)} %copy.146), kind=kOutput, calls=%fused_computation.57 | convolution fusion | flops 268435456 | bytes 5308416 | tf_op jit(solution)/shard_map/transpose | solution.py:61
  680.8 453.2 %fusion.45 = f32[32,4,3,3,3]{0,1,4,3,2:T(4,128)S(1)} fusion(bf16[4,1,4,66,514]{0,1,4,3,2:T(2,128)(2,1)} %copy.142, bf16[32,1,2,64,512]{0,1,4,3,2:T(2,128)(2,1)} %copy.143), kind=kOutput, calls=%fused_computation.56 | convolution fusion | flops 452984832 | bytes 5293696 | tf_op jit(solution)/shard_map/transpose | solution.py:62
  1133.9 40.2 %psum.14 = f32[32,4,3,3,3]{0,1,4,3,2:T(4,128)S(1)} all-reduce(f32[32,4,3,3,3]{0,1,4,3,2:T(4,128)S(1)} %fusion.45), channel_id=1, replica_groups=mesh['space'=8,'filt'=4] {'space','filt'}, use_global_device_ids=true, to_apply=%region_0.1 | all-reduce | flops 3456 | bytes 27648 | tf_op jit(solution)/shard_map/psum | solution.py:96
  (58 shorter events, 62.3 us)
Async XLA Ops:
  7.2 228.5 %copy-start = (bf16[64,32,2,2,2]{0,4,3,2,1:T(2,128)(2,1)S(1)}, bf16[64,32,2,2,2]{0,4,3,2,1:T(2,128)(2,1)}, u32[]{:S(2)}) copy-start(bf16[64,32,2,2,2]{0,4,3,2,1:T(2,128)(2,1)} %param.6) | copy-start | bytes 98308
  8.3 7.1 collective-permute-start
  12.1 7.7 collective-permute-start.1
  19.8 11.2 collective-permute-start.2
  23.0 8.1 collective-permute-start.3
  26.8 222.0 %all-to-all-start.2 = ((bf16[16,8,16,256]{3,2,0,1:T(8,128)(2,1)}), bf16[16,8,16,256]{3,2,0,1:T(8,128)(2,1)}, u32[]{:S(2)}, u32[]{:S(2)}) async-start(bf16[16,8,16,256]{3,2,0,1:T(8,128)(2,1)} %copy.152), calls=%async_computation.2 | async-start | bytes 2097152 | tf_op jit(solution)/shard_map/all_to_all | solution.py:88
  55.9 25.6 %copy-start.5 = (bf16[32,4,3,3,3]{0,1,4,3,2:T(4,128)(2,1)S(1)}, bf16[32,4,3,3,3]{0,1,4,3,2:T(4,128)(2,1)}, u32[]{:S(2)}) copy-start(bf16[32,4,3,3,3]{0,1,4,3,2:T(4,128)(2,1)} %param.5) | copy-start | bytes 20740
  55.9 25.6 %copy-start.6 = (pred[8,65]{0,1:T(8,128)(4,1)S(1)}, pred[8,65]{0,1:T(8,128)(4,1)}, u32[]{:S(2)}) copy-start(pred[8,65]{0,1:T(8,128)(4,1)} %constant.34) | copy-start | bytes 1564
  248.8 19.0 %all-to-all-start = ((bf16[64,1,32,256]{3,2,1,0:T(8,128)(2,1)}), bf16[64,1,32,256]{3,2,1,0:T(8,128)(2,1)S(1)}, u32[]{:S(2)}, u32[]{:S(2)}) async-start(bf16[64,1,32,256]{3,2,1,0:T(8,128)(2,1)} %copy.127), calls=%async_computation | async-start | bytes 2097152 | tf_op jit(solution)/shard_map/all_to_all | solution.py:80
  267.8 3.5 copy-start.3
  267.8 145.9 %all-to-all-start.3 = ((bf16[16,1,128,256]{3,0,1,2:T(8,128)(2,1)}), bf16[16,1,128,256]{3,0,1,2:T(8,128)(2,1)S(1)}, u32[]{:S(2)}, u32[]{:S(2)}) async-start(bf16[16,1,128,256]{3,0,1,2:T(8,128)(2,1)} %copy.134), calls=%async_computation.3 | async-start | bytes 2097152 | tf_op jit(solution)/shard_map/all_to_all | solution.py:87
  299.8 16.6 %copy-start.2 = (bf16[4,1,4,66,514]{4,3,2,0,1:T(8,128)(2,1)S(1)}, bf16[4,1,4,66,514]{4,3,2,0,1:T(8,128)(2,1)}, u32[]{:S(2)}) copy-start(bf16[4,1,4,66,514]{4,3,2,0,1:T(8,128)(2,1)} %get-tuple-element.23) | copy-start | bytes 3256708
  412.1 19.0 %copy-start.4 = (pred[8,66]{0,1:T(8,128)(4,1)S(1)}, pred[8,66]{0,1:T(8,128)(4,1)}, u32[]{:S(2)}) copy-start(pred[8,66]{0,1:T(8,128)(4,1)} %constant.36) | copy-start | bytes 1588
  413.7 762.6 %all-to-all-start.1 = ((bf16[16,1,128,256]{3,0,1,2:T(8,128)(2,1)}), bf16[16,1,128,256]{3,0,1,2:T(8,128)(2,1)}, u32[]{:S(2)}, u32[]{:S(2)}) async-start(bf16[16,1,128,256]{3,0,1,2:T(8,128)(2,1)} %copy.129), calls=%async_computation.1 | async-start | bytes 2097152 | tf_op jit(solution)/shard_map/all_to_all | solution.py:79
  419.0 755.9 %all-reduce.3.cloned.1.call-start = ((), (), s32[]{:S(2)}) async-start(), calls=%async_computation.4 | async-start | bytes 262144 | tf_op jit(solution)/shard_map/psum | solution.py:96
  680.8 498.4 %copy-start.1 = (bf16[64,32,2,2,2]{0,4,3,2,1:T(2,128)(2,1)S(1)}, bf16[64,32,2,2,2]{0,4,3,2,1:T(2,128)(2,1)}, u32[]{:S(2)}) copy-start(bf16[64,32,2,2,2]{0,4,3,2,1:T(2,128)(2,1)} %param.6) | copy-start | bytes 98308
Sparse Core Ops, SparseCore 0:
  680.9 121.5 all-reduce.2
where the time goes:
time: 1210 us; the launch traced here: 1190 us
  matrix products  620 us (51%)
  local copies, waits for them, and re-layouts  430 us (36%)
  blocking collectives  40.2 us (3%)
  other arithmetic  37.4 us (3%)
  starting transfers between devices  27.5 us (2%)
  waiting for transfers between devices  16.4 us (1%)
  between operations  14.7 us (1%)
    transpose x1, matrix products, kernel_grads(): convolve(framed[:, None], steered[:, None], (1, 1, 1), 'VALID')  453 us
    convert_element_type x7, local copies, waits for them, and re-layouts, first_layer(): jnp.where(first_out > 0, first_out, SLOPE * first_out).astype(jnp.bfloat16)  131 us
    conv_general_dilated x7, local copies, waits for them, and re-layouts, convolve(): lax.conv_general_dilated(left_operand, right_operand, strides, padding, l...  111 us
    conv_general_dilated x3, matrix products, convolve(): lax.conv_general_dilated(left_operand, right_operand, strides, padding, l...  108 us
    broadcast_in_dim x1, local copies, waits for them, and re-layouts, kernel_grads(): framed[:, None]  94.3 us
    convert_element_type x1, local copies, waits for them, and re-layouts, kernel_grads(): steered = (back_flow * slopes).astype(jnp.bfloat16)  61.6 us
    transpose x1, matrix products, kernel_grads(): second_term = convolve(active[:, None], gradient[:, None], (1, 1, 1), 'VA...  59.5 us
    psum x1, blocking collectives, shards(): lax.psum((first_term, second_term), ('space', 'filt'))  40.2 us
  transfers between devices with their start and end apart: 9, of which 3 were waited for; matrix products, arithmetic and copies ran while one was open for 91% of the time, Pallas kernels for 0%

commit v1 on v0

v1 whole, which is shorter than its diff:
```python
import jax
import jax.numpy as jnp
import numpy as np
from jax import lax
from jax.experimental import pallas as pl
from jax.experimental.pallas import tpu as pltpu
from jax.sharding import PartitionSpec as P

SLOPE = 0.3
GROUP = 4
TAPS = 128


def tap_table(channels):
    table = np.zeros((TAPS, 8, 4, 4, 4, channels), np.float32)
    for cell in range(8):
        a, b, g = cell // 4, (cell // 2) % 2, cell % 2
        for tap in range(channels * 27):
            c, i, j, k = tap // 27, (tap // 9) % 3, (tap // 3) % 3, tap % 3
            table[tap, cell, g + k, b + j, a + i, c] = 1.0
    return table.reshape(TAPS, 8 * 64 * channels)


def dot(left, right, dims=((1,), (0,)), precision=None):
    return lax.dot_general(left, right, (dims, ((), ())), precision=precision, preferred_element_type=jnp.float32)


def section(vol, before, after, above, below, up, taps, table, second, pooled, grads, cells, first_mat, back_mat, g_first, g_second):
    channels, planes, rows, cols = vol.shape
    window = channels * 4
    half = cols // 2
    lanes = half // 128
    filters = taps.shape[0]
    depth = 8 * filters
    source = lax.broadcasted_iota(jnp.int32, (cols, 4 * half), 0)
    target = lax.broadcasted_iota(jnp.int32, (cols, 4 * half), 1)
    pick = (source == 2 * lax.rem(target, half) + lax.div(target, half) - 1).astype(jnp.float32).astype(jnp.bfloat16)

    for dz in range(4):
        for c in range(channels):
            plane = before[c, 0] if dz == 0 else after[c, 0] if dz == 3 else vol[c, dz - 1]
            spread = dot(plane, pick)
            for lane in range(4 * lanes):
                cells[lane, pl.ds(window + dz * channels + c, rows, stride=window), :] = spread[:, lane * 128:(lane + 1) * 128]
    for edge, at in ((above, 0), (below, window * (rows + 1))):
        spread = dot(edge[...], pick)
        for lane in range(4 * lanes):
            cells[lane, at:at + window, :] = spread[:, lane * 128:(lane + 1) * 128]

    size = 16 * channels * 4
    for cell in range(8):
        first_mat[cell * filters:(cell + 1) * filters, :] = dot(taps[...], table[:, cell * size:(cell + 1) * size]).astype(jnp.bfloat16)
    back_mat[...] = second[...].astype(jnp.float32).T.astype(jnp.bfloat16)
    g_first[...] = jnp.zeros_like(g_first)
    g_second[...] = jnp.zeros_like(g_second)
    per_part = up.shape[2] // (GROUP * half)

    def step(index, carry):
        columns = []
        for y in range(GROUP):
            start = pl.multiple_of((index * GROUP + y) * 2 * window, 2 * window)
            tiles = [
                jnp.concatenate(
                    [cells[dx * lanes + lane, pl.ds(start, 4 * window), :].astype(jnp.bfloat16) for lane in range(lanes)], axis=1
                )
                for dx in range(4)
            ]
            columns.append(jnp.concatenate(tiles, axis=0))
        patches = jnp.concatenate(columns, axis=1)
        part = index // per_part
        span = pl.ds(pl.multiple_of((index % per_part) * GROUP * half, GROUP * half), GROUP * half)
        first_out = dot(first_mat[...], patches)
        active = jnp.where(first_out > 0, first_out, SLOPE * first_out).astype(jnp.bfloat16)
        pooled[part, :, span] = dot(second[...], active).astype(jnp.bfloat16)
        gradient = up[part, :, span]
        back_flow = dot(back_mat[...], gradient)
        steered = (back_flow * jnp.where(active.astype(jnp.float32) > 0, 1.0, SLOPE)).astype(jnp.bfloat16)
        g_second[...] += dot(gradient, active, ((1,), (1,)))
        g_first[...] += dot(steered, patches, ((1,), (1,)))
        return carry

    lax.fori_loop(0, rows // 2 // GROUP, step, 0)
    outputs = second.shape[0]
    grads[0:outputs, :] = g_second[...]
    total = jnp.zeros((filters, TAPS), jnp.float32)
    for cell in range(8):
        part = table[:, cell * size:(cell + 1) * size].astype(jnp.float32)
        total += dot(g_first[cell * filters:(cell + 1) * filters, :], part, ((1,), (1,)), lax.Precision.HIGHEST)
    grads[outputs:outputs + filters, :] = jnp.concatenate([total, jnp.zeros((filters, depth - TAPS), jnp.float32)], axis=1)


def halo(cells, axis, dim):
    count = lax.axis_size(axis)
    ends = count - 1
    head = lax.slice_in_dim(cells, 0, 1, axis=dim)
    tail = lax.slice_in_dim(cells, cells.shape[dim] - 1, cells.shape[dim], axis=dim)
    return (
        lax.ppermute(tail, axis, [(i, i + 1) for i in range(ends)]),
        lax.ppermute(head, axis, [(i + 1, i) for i in range(ends)]),
    )


def shards(volume, first_kernel, second_kernel, upstream):
    space, groups = lax.axis_size("space"), lax.axis_size("filt")
    channels, planes, rows, cols = volume.shape
    filters, outputs = first_kernel.shape[0], second_kernel.shape[0]
    group_out, depth_out, band = upstream.shape
    parts = space // groups
    half = cols // 2

    before, after = halo(volume, "space", 1)
    edges = lambda at: jnp.concatenate([a[:, :, at] for a in (before, volume, after)], axis=1).transpose(1, 0, 2)
    ends = groups - 1
    above = lax.ppermute(edges(rows - 1), "filt", [(i, i + 1) for i in range(ends)]).reshape(4 * channels, cols)
    below = lax.ppermute(edges(0), "filt", [(i + 1, i) for i in range(ends)]).reshape(4 * channels, cols)

    sent = upstream.transpose(1, 0, 2)
    sent = lax.all_to_all(sent, "space", 0, 0, tiled=True).reshape(groups, parts, group_out, band)
    sent = lax.all_to_all(sent, "filt", 0, 0, tiled=True)
    up = sent.transpose(1, 0, 2, 3).reshape(parts, outputs, band)

    taps = jnp.pad(first_kernel.reshape(filters, channels * 27), ((0, 0), (0, TAPS - channels * 27)))
    table = jnp.asarray(tap_table(channels), jnp.bfloat16)
    second = second_kernel.transpose(0, 2, 3, 4, 1).reshape(outputs, 8 * filters)
    window = 4 * channels
    vmem = pl.BlockSpec(memory_space=pltpu.VMEM)
    pooled, grads = pl.pallas_call(
        section,
        out_shape=(
            jax.ShapeDtypeStruct((parts, outputs, band), jnp.bfloat16),
            jax.ShapeDtypeStruct((outputs + filters, 8 * filters), jnp.float32),
        ),
        in_specs=[vmem] * 9,
        out_specs=(vmem, vmem),
        scratch_shapes=[
            pltpu.VMEM((4 * half // 128, window * (rows + 2), 128), jnp.float32),
            pltpu.VMEM((8 * filters, 16 * window), jnp.bfloat16),
            pltpu.VMEM((8 * filters, outputs), jnp.bfloat16),
            pltpu.VMEM((8 * filters, 16 * window), jnp.float32),
            pltpu.VMEM((outputs, 8 * filters), jnp.float32),
        ],
        compiler_params=pltpu.CompilerParams(vmem_limit_bytes=48 * 2**20),
        cost_estimate=pl.CostEstimate(flops=6 * 10**9, bytes_accessed=4 * 10**6, transcendentals=0),
        name="section",
    )(volume, before, after, above, below, up, taps, table, second)

    moved = pooled.reshape(parts, groups, group_out, band).transpose(1, 0, 2, 3)
    moved = lax.all_to_all(moved, "filt", 0, 0, tiled=True).reshape(space, group_out, band)
    moved = lax.all_to_all(moved, "space", 0, 0, tiled=True)
    grads = lax.psum(grads, ("space", "filt"))
    offset = lax.axis_index("filt") * (filters // groups)
    own = filters // groups
    grad_first = lax.dynamic_slice(grads, (outputs + offset, 0), (own, channels * 27)).reshape(own, channels, 3, 3, 3)
    grad_second = lax.dynamic_slice_in_dim(grads[:outputs].reshape(outputs, 2, 2, 2, filters), offset, own, 4).transpose(0, 4, 1, 2, 3)
    return (moved.transpose(1, 0, 2), grad_first, grad_second)


def solution(mesh):
    in_specs = (P(None, "space", "filt", None), P(), P(), P("filt", None, "space"))
    out_specs = (
        P("filt", None, "space"),
        P("filt", None, None, None, None),
        P(None, "filt", None, None, None),
    )
    return jax.shard_map(shards, mesh=mesh, in_specs=in_specs, out_specs=out_specs, check_vma=False)
```

time: 1210 us -> 240 us (0.20); the launches traced: 1190 us -> 238 us
  matrix products: 620 us -> 0 us
  local copies, waits for them, and re-layouts: 430 us -> 9.53 us
  waiting for transfers between devices: 16.4 us -> 156 us
  other arithmetic: 37.4 us -> 0.07 us
  blocking collectives: 40.2 us -> 15.2 us
  Pallas kernels: 0 us -> 13.5 us
    transpose x2 -> x0, matrix products: 513 us -> none  [the longest x1 453 us: kernel_grads(): convolve(framed[:, None], steered[:, None], (1, 1, 1), 'VALID')]
    convert_element_type x10 -> x0, local copies, waits for them, and re-layouts: 195 us -> none  [the longest x7 131 us: first_layer(): jnp.where(first_out > 0, first_out, SLOPE * first_out).astype(jnp.bfloat16)]
    psum x1, waiting for transfers between devices: 0.01 us -> 131 us  [shards(): grads = lax.psum(grads, ('space', 'filt'))]
    conv_general_dilated x7 -> x0, local copies, waits for them, and re-layouts: 111 us -> none  [convolve(): lax.conv_general_dilated(left_operand, right_operand, strides, padding, l...]
    conv_general_dilated x3 -> x0, matrix products: 108 us -> none  [convolve(): lax.conv_general_dilated(left_operand, right_operand, strides, padding, l...]
    broadcast_in_dim x4 -> x0, local copies, waits for them, and re-layouts: 103 us -> none  [the longest x1 94.3 us: kernel_grads(): framed[:, None]]
    psum x1 -> x0, blocking collectives: 40.2 us -> none  [shards(): lax.psum((first_term, second_term), ('space', 'filt'))]
    convert_element_type x2 -> x0, other arithmetic: 34.8 us -> none  [the longest x1 25.5 us: first_layer(): jnp.where(first_out > 0, first_out, SLOPE * first_out).astype(jnp.bfloat16)]
  transfers between devices with their start and end apart: 9 -> 8, of which waited for: 3 -> 4; matrix products, arithmetic and copies ran while one was open for 91% -> 1% of each run, Pallas kernels for 0% -> 0%
where the time goes in v1:
time: 240 us; the launch traced here: 238 us
  waiting for transfers between devices  156 us (65%)
  starting transfers between devices  28.7 us (12%)
  blocking collectives  15.2 us (6%)
  between operations  14.3 us (6%)
  Pallas kernels  13.5 us (6%)
  local copies, waits for them, and re-layouts  9.53 us (4%)
    psum x1, waiting for transfers between devices, shards(): grads = lax.psum(grads, ('space', 'filt'))  131 us
    all_to_all x1, waiting for transfers between devices, shards(): lax.all_to_all(sent, 'space', 0, 0, tiled=True)  17.7 us
    all_to_all x1, blocking collectives, shards(): lax.all_to_all(moved, 'filt', 0, 0, tiled=True)  15.2 us
    pallas_call x1, Pallas kernels, shards(): pl.pallas_call(section, out_shape=(jax.ShapeDtypeStruct((parts, outputs,...  13.5 us
    all_to_all x1, starting transfers between devices, shards(): moved = lax.all_to_all(moved, 'space', 0, 0, tiled=True)  8.87 us
    unnamed x15, local copies, waits for them, and re-layouts  7.25 us
    ppermute x1, waiting for transfers between devices, shards(): lax.ppermute(edges(0), 'filt', [(i + 1, i) for i in range(ends)])  5.97 us
    all_to_all x1, starting transfers between devices, shards(): lax.all_to_all(sent, 'space', 0, 0, tiled=True)  5.77 us
  transfers between devices with their start and end apart: 8, of which 4 were waited for; matrix products, arithmetic and copies ran while one was open for 1% of the time, Pallas kernels for 0%

profile of v1, /device:TPU:9, one launch (start us, length us, event | category | flops | bytes accessed | tf_op | source)
XLA Modules:
  0.0 237.6 jit_solution(11151163843921235790)
XLA Ops:
  7.2 2.8 %copy.60 = bf16[16,8,4096]{2,0,1:T(8,128)(2,1)} copy(bf16[16,8,4096]{2,1,0:T(8,128)(2,1)} %param.8) | data formatting | bytes 2097152 | tf_op args[3]
  9.9 5.8 %all-to-all-start = ((bf16[8,16,4096]{2,1,0:T(8,128)(2,1)}), bf16[8,16,4096]{2,1,0:T(8,128)(2,1)}, u32[]{:S(2)}, u32[]{:S(2)}) async-start(bf16[8,16,4096]{2,1,0:T(8,128)(2,1)} %bitcast.36), calls=%async_computation | async-start | bytes 2097152 | tf_op jit(solution)/shard_map/all_to_all | solution.py:118
  15.8 3.3 %collective-permute-start = (bf16[4,1,64,512]{3,2,1,0:T(8,128)(2,1)S(1)}, bf16[4,1,64,512]{3,2,1,0:T(8,128)(2,1)S(1)}, u32[]{:S(2)}, u32[]{:S(2)}) collective-permute-start(bf16[4,1,64,512]{3,2,1,0:T(8,128)(2,1)S(1)} %get-tuple-element.16), channel_id=1, source_target_pairs={{0,4},{4,8},{8,12},{12,16},{16,20},{20,24},{24,28},{1,5},{5,9},{9,... | collective-permute-start | bytes 786440 | tf_op jit(solution)/shard_map/ppermute | solution.py:98
  19.1 1.9 collective-permute-start.1
  21.0 17.7 %all-to-all-done = bf16[8,16,4096]{2,1,0:T(8,128)(2,1)} async-done(((bf16[8,16,4096]{2,1,0:T(8,128)(2,1)}), bf16[8,16,4096]{2,1,0:T(8,128)(2,1)}, u32[]{:S(2)}, u32[]{:S(2)}) %all-to-all-start) | async-done | bytes 1048608 | tf_op jit(solution)/shard_map/all_to_all | solution.py:118
  38.8 3.5 %all-to-all-start.1 = ((bf16[4,2,16,4096]{3,2,1,0:T(8,128)(2,1)}), bf16[4,2,16,4096]{3,2,1,0:T(8,128)(2,1)S(1)}, u32[]{:S(2)}, u32[]{:S(2)}) async-start(bf16[4,2,16,4096]{3,2,1,0:T(8,128)(2,1)} %bitcast.7), calls=%async_computation.1 | async-start | bytes 2097152 | tf_op jit(solution)/shard_map/all_to_all | solution.py:119
  42.4 0.9 collective-permute-done.1.after
  43.4 1.3 collective-permute-start.3
  44.7 4.0 %collective-permute-start.2 = (bf16[4,4,512]{2,0,1:T(4,128)(2,1)S(1)}, bf16[4,4,512]{2,0,1:T(4,128)(2,1)S(1)}, u32[]{:S(2)}, u32[]{:S(2)}) collective-permute-start(bf16[4,4,512]{2,0,1:T(4,128)(2,1)S(1)} %maximum_bitcast_fusion), channel_id=1, source_target_pairs={{0,1},{1,2},{2,3},{4,5},{5,6},{6,7},{8,9},{9,10},{10,11},{12,13},{... | collective-permute-start | bytes 49160 | tf_op jit(solution)/shard_map/ppermute | solution.py:114
  48.9 0.6 copy-done.3
  49.7 6.0 %collective-permute-done.3 = bf16[4,4,512]{2,0,1:T(4,128)(2,1)S(1)} collective-permute-done((bf16[4,4,512]{2,0,1:T(4,128)(2,1)S(1)}, bf16[4,4,512]{2,0,1:T(4,128)(2,1)S(1)}, u32[]{:S(2)}, u32[]{:S(2)}) %collective-permute-start.3) | collective-permute-done | bytes 16416 | tf_op jit(solution)/shard_map/ppermute | solution.py:115
  55.8 1.0 copy-done.1
  56.8 13.5 %section.1 = (bf16[2,64,4096]{2,1,0:T(8,128)(2,1)S(1)}, f32[96,256]{1,0:T(8,128)}) custom-call(bf16[4,2,64,512]{3,2,1,0:T(8,128)(2,1)S(1)} %copy-done, bf16[4,1,64,512]{3,2,1,0:T(8,128)(2,1)S(1)} %collective-permute-done.before, bf16[4,1,64,512]{3,2,1,0:T(8,128)(2,1)S(1)} %collective-permute-done.1.after, bf16[16,512]{1,0:T(8,128)(2,1)S(1)} %reshape.36.above, ...), custom_call_target="tpu_custom_call" | custom-call | flops 6000000000 | bytes 4000000 | tf_op jit(solution)/shard_map/section/pallas_call | solution.py:127
  70.3 15.2 %all_to_all.20 = bf16[4,2,16,4096]{3,2,1,0:T(8,128)(2,1)} all-to-all(bf16[4,2,16,4096]{3,2,1,0:T(8,128)(2,1)S(1)} %bitcast.43), channel_id=1, replica_groups=mesh['space'=8,'filt'=4] {'filt'}, dimensions={0} | all-to-all | bytes 2097152 | tf_op jit(solution)/shard_map/all_to_all | solution.py:148
  85.6 8.9 %all-to-all-start.3 = ((bf16[8,16,4096]{2,1,0:T(8,128)(2,1)}), bf16[8,16,4096]{2,1,0:T(8,128)(2,1)S(1)}, u32[]{:S(2)}, u32[]{:S(2)}) async-start(bf16[8,16,4096]{2,1,0:T(8,128)(2,1)} %bitcast.14), calls=%async_computation.3 | async-start | bytes 2097152 | tf_op jit(solution)/shard_map/all_to_all | solution.py:149
  94.4 0.7 all-reduce.3.cloned.1.call-update
  95.2 131.0 %all-reduce.3.cloned.1.call-done = f32[96,256]{1,0:T(8,128)} async-done(((f32[96,256]{1,0:T(8,128)}), f32[96,256]{1,0:T(8,128)}) %all-reduce.3.cloned.1.call-update) | async-done | bytes 98320 | tf_op jit(solution)/shard_map/psum | solution.py:150
  226.1 0.7 constant_dynamic-slice_fusion
  226.8 0.1 copy.48
  226.9 0.6 copy.51
  227.6 0.8 slice-done
  228.4 0.1 copy.49
  228.5 0.6 copy.52
  229.2 1.6 copy.50
  (34 shorter events, 0.7 us)
Async XLA Ops:
  9.9 5.8 %copy-start = (bf16[4,2,64,512]{3,2,1,0:T(8,128)(2,1)S(1)}, bf16[4,2,64,512]{3,2,1,0:T(8,128)(2,1)}, u32[]{:S(2)}) copy-start(bf16[4,2,64,512]{3,2,1,0:T(8,128)(2,1)} %vol.1) | copy-start | bytes 1572868
  9.9 28.8 %all-to-all-start = ((bf16[8,16,4096]{2,1,0:T(8,128)(2,1)}), bf16[8,16,4096]{2,1,0:T(8,128)(2,1)}, u32[]{:S(2)}, u32[]{:S(2)}) async-start(bf16[8,16,4096]{2,1,0:T(8,128)(2,1)} %bitcast.36), calls=%async_computation | async-start | bytes 2097152 | tf_op jit(solution)/shard_map/all_to_all | solution.py:118
  15.8 26.6 %collective-permute-start = (bf16[4,1,64,512]{3,2,1,0:T(8,128)(2,1)S(1)}, bf16[4,1,64,512]{3,2,1,0:T(8,128)(2,1)S(1)}, u32[]{:S(2)}, u32[]{:S(2)}) collective-permute-start(bf16[4,1,64,512]{3,2,1,0:T(8,128)(2,1)S(1)} %get-tuple-element.16), channel_id=1, source_target_pairs={{0,4},{4,8},{8,12},{12,16},{16,20},{20,24},{24,28},{1,5},{5,9},{9,... | collective-permute-start | bytes 786440 | tf_op jit(solution)/shard_map/ppermute | solution.py:98
  19.1 24.2 %collective-permute-start.1 = (bf16[4,1,64,512]{3,2,1,0:T(8,128)(2,1)S(1)}, bf16[4,1,64,512]{3,2,1,0:T(8,128)(2,1)S(1)}, u32[]{:S(2)}, u32[]{:S(2)}) collective-permute-start(bf16[4,1,64,512]{3,2,1,0:T(8,128)(2,1)S(1)} %get-tuple-element.15), channel_id=1, source_target_pairs={{4,0},{8,4},{12,8},{16,12},{20,16},{24,20},{28,24},{5,1},{9,5},{13... | collective-permute-start | bytes 786440 | tf_op jit(solution)/shard_map/ppermute | solution.py:99
  38.8 16.9 %all-to-all-start.1 = ((bf16[4,2,16,4096]{3,2,1,0:T(8,128)(2,1)}), bf16[4,2,16,4096]{3,2,1,0:T(8,128)(2,1)S(1)}, u32[]{:S(2)}, u32[]{:S(2)}) async-start(bf16[4,2,16,4096]{3,2,1,0:T(8,128)(2,1)} %bitcast.7), calls=%async_computation.1 | async-start | bytes 2097152 | tf_op jit(solution)/shard_map/all_to_all | solution.py:119
  42.4 6.3 %copy-start.2 = (bf16[64,32,2,2,2]{0,4,3,2,1:T(2,128)(2,1)S(1)}, bf16[64,32,2,2,2]{0,4,3,2,1:T(2,128)(2,1)}, u32[]{:S(2)}) copy-start(bf16[64,32,2,2,2]{0,4,3,2,1:T(2,128)(2,1)} %param.7) | copy-start | bytes 98308
  43.4 12.2 %collective-permute-start.3 = (bf16[4,4,512]{2,0,1:T(4,128)(2,1)S(1)}, bf16[4,4,512]{2,0,1:T(4,128)(2,1)S(1)}, u32[]{:S(2)}, u32[]{:S(2)}) collective-permute-start(bf16[4,4,512]{2,0,1:T(4,128)(2,1)S(1)} %maximum_bitcast_fusion.1), channel_id=1, source_target_pairs={{1,0},{2,1},{3,2},{5,4},{6,5},{7,6},{9,8},{10,9},{11,10},{13,12},{... | collective-permute-start | bytes 49160 | tf_op jit(solution)/shard_map/ppermute | solution.py:115
  44.7 10.9 %collective-permute-start.2 = (bf16[4,4,512]{2,0,1:T(4,128)(2,1)S(1)}, bf16[4,4,512]{2,0,1:T(4,128)(2,1)S(1)}, u32[]{:S(2)}, u32[]{:S(2)}) collective-permute-start(bf16[4,4,512]{2,0,1:T(4,128)(2,1)S(1)} %maximum_bitcast_fusion), channel_id=1, source_target_pairs={{0,1},{1,2},{2,3},{4,5},{5,6},{6,7},{8,9},{9,10},{10,11},{12,13},{... | collective-permute-start | bytes 49160 | tf_op jit(solution)/shard_map/ppermute | solution.py:114
  48.8 0.7 copy-start.3
  55.7 1.0 copy-start.1
  85.6 143.6 %all-to-all-start.3 = ((bf16[8,16,4096]{2,1,0:T(8,128)(2,1)}), bf16[8,16,4096]{2,1,0:T(8,128)(2,1)S(1)}, u32[]{:S(2)}, u32[]{:S(2)}) async-start(bf16[8,16,4096]{2,1,0:T(8,128)(2,1)} %bitcast.14), calls=%async_computation.3 | async-start | bytes 2097152 | tf_op jit(solution)/shard_map/all_to_all | solution.py:149
  94.4 131.7 %all-reduce.3.cloned.1.call-start = ((), (), s32[]{:S(2)}) async-start(), calls=%async_computation.4 | async-start | bytes 196608 | tf_op jit(solution)/shard_map/psum | solution.py:150
  227.6 0.8 slice-start
Sparse Core Ops, SparseCore 0:
  101.4 124.6 all-reduce.2

commit v2 on v1

v2 whole, which is shorter than its diff:
```python
import functools

import jax
import jax.numpy as jnp
import numpy as np
from jax import lax
from jax.experimental import pallas as pl
from jax.experimental.pallas import tpu as pltpu
from jax.sharding import PartitionSpec as P

SLOPE = 0.3
GROUP = 4
TAPS = 128
MESH = pl.DeviceIdType.MESH


def tap_table(channels):
    table = np.zeros((TAPS, 8, 4, 4, 4, channels), np.float32)
    for cell in range(8):
        a, b, g = cell // 4, (cell // 2) % 2, cell % 2
        for tap in range(channels * 27):
            c, i, j, k = tap // 27, (tap // 9) % 3, (tap // 3) % 3, tap % 3
            table[tap, cell, g + k, b + j, a + i, c] = 1.0
    return table.reshape(TAPS, 8 * 64 * channels)


def dot(left, right, dims=((1,), (0,)), precision=None):
    return lax.dot_general(left, right, (dims, ((), ())), precision=precision, preferred_element_type=jnp.float32)


def section(vol, before, after, above, below, up, taps, table, second, pooled, grads, cells, first_mat, back_mat, g_first, g_second):
    channels, planes, rows, cols = vol.shape
    window = channels * 4
    half = cols // 2
    lanes = half // 128
    filters = taps.shape[0]
    depth = 8 * filters
    source = lax.broadcasted_iota(jnp.int32, (cols, 4 * half), 0)
    target = lax.broadcasted_iota(jnp.int32, (cols, 4 * half), 1)
    pick = (source == 2 * lax.rem(target, half) + lax.div(target, half) - 1).astype(jnp.float32).astype(jnp.bfloat16)

    for dz in range(4):
        for c in range(channels):
            plane = before[c] if dz == 0 else after[c] if dz == 3 else vol[c, dz - 1]
            spread = dot(plane, pick)
            for lane in range(4 * lanes):
                cells[lane, pl.ds(window + dz * channels + c, rows, stride=window), :] = spread[:, lane * 128:(lane + 1) * 128]
    for edge, at in ((above, 0), (below, window * (rows + 1))):
        spread = dot(edge[...], pick)
        for lane in range(4 * lanes):
            cells[lane, at:at + window, :] = spread[:, lane * 128:(lane + 1) * 128]

    size = 16 * channels * 4
    for cell in range(8):
        first_mat[cell * filters:(cell + 1) * filters, :] = dot(taps[...], table[:, cell * size:(cell + 1) * size]).astype(jnp.bfloat16)
    back_mat[...] = second[...].astype(jnp.float32).T.astype(jnp.bfloat16)
    g_first[...] = jnp.zeros_like(g_first)
    g_second[...] = jnp.zeros_like(g_second)
    groups, _, group_out, band = up.shape
    own = filters // groups
    outputs = second.shape[0]
    per_part = band // (GROUP * half)

    def step(index, carry):
        columns = []
        for y in range(GROUP):
            start = pl.multiple_of((index * GROUP + y) * 2 * window, 2 * window)
            tiles = [
                jnp.concatenate(
                    [cells[dx * lanes + lane, pl.ds(start, 4 * window), :].astype(jnp.bfloat16) for lane in range(lanes)], axis=1
                )
                for dx in range(4)
            ]
            columns.append(jnp.concatenate(tiles, axis=0))
        patches = jnp.concatenate(columns, axis=1)
        part = index // per_part
        span = pl.ds(pl.multiple_of((index % per_part) * GROUP * half, GROUP * half), GROUP * half)
        first_out = dot(first_mat[...], patches)
        active = jnp.where(first_out > 0, first_out, SLOPE * first_out).astype(jnp.bfloat16)
        pooled_tile = dot(second[...], active).astype(jnp.bfloat16)
        for group in range(groups):
            pooled[group, part, :, span] = pooled_tile[group * group_out:(group + 1) * group_out]
        gradient = jnp.concatenate([up[group, part, :, span] for group in range(groups)], axis=0)
        back_flow = dot(back_mat[...], gradient)
        steered = (back_flow * jnp.where(active.astype(jnp.float32) > 0, 1.0, SLOPE)).astype(jnp.bfloat16)
        g_second[...] += dot(active, gradient, ((1,), (1,)))
        g_first[...] += dot(steered, patches, ((1,), (1,)))
        return carry

    lax.fori_loop(0, rows // 2 // GROUP, step, 0)
    grads[...] = jnp.zeros_like(grads)
    total = jnp.zeros((filters, TAPS), jnp.float32)
    for cell in range(8):
        part = table[:, cell * size:(cell + 1) * size].astype(jnp.float32)
        total += dot(g_first[cell * filters:(cell + 1) * filters, :], part, ((1,), (1,)), lax.Precision.HIGHEST)
    for group in range(groups):
        for cell in range(8):
            first = cell * filters + group * own
            grads[group, cell, :, 0:outputs] = g_second[first:first + own, :]
        grads[group, 8, :, :] = total[group * own:(group + 1) * own]


def greet(space, groups, s, f):
    barrier = pltpu.get_barrier_semaphore()
    for d in range(1, space):
        pl.semaphore_signal(barrier, inc=1, device_id=(lax.rem(s + d, space), f), device_id_type=MESH)
    for e in range(1, groups):
        pl.semaphore_signal(barrier, inc=1, device_id=(s, lax.rem(f + e, groups)), device_id_type=MESH)
    pl.semaphore_wait(barrier, space + groups - 2)


def push(source, target, sems, index, device):
    send, recv = sems
    return pltpu.make_async_remote_copy(
        src_ref=source, dst_ref=target, send_sem=send.at[index], recv_sem=recv.at[index], device_id=device, device_id_type=MESH
    )


def when_sent(there, here, copy):
    @pl.when(there)
    def _():
        copy.wait_send()

    @pl.when(here)
    def _():
        copy.wait_recv()


def halo(s, count, ahead, back, filled, emptied):
    @pl.when(s < count - 1)
    def _():
        ahead.start()

    @pl.when(s > 0)
    def _():
        back.start()

    @pl.when(s == 0)
    def _():
        filled[...] = jnp.zeros_like(filled)

    @pl.when(s == count - 1)
    def _():
        emptied[...] = jnp.zeros_like(emptied)


def collect(space, groups, vol, up, before, after, above, below, up_out, mid, tail, head, h_send, h_recv, z_send, z_recv, f_send, f_recv):
    s, f = lax.axis_index("space"), lax.axis_index("filt")
    channels, planes, rows, cols = vol.shape
    parts = space // groups
    greet(space, groups, s, f)
    sems = (h_send, h_recv)
    ahead = push(vol.at[:, planes - 1], before, sems, 0, (jnp.minimum(s + 1, space - 1), f))
    back = push(vol.at[:, 0], after, sems, 1, (jnp.maximum(s - 1, 0), f))
    halo(s, space, ahead, back, before, after)
    moves = []
    for d in range(1, space):
        peer = lax.rem(s + d, space)
        moves.append(push(up.at[peer], mid.at[s], (z_send, z_recv), d, (peer, f)))
        moves[-1].start()
    mid[s] = up[s]
    when_sent(s < space - 1, s > 0, ahead)
    when_sent(s > 0, s < space - 1, back)

    def edge(row):
        lines = [
            (before[c] if dz == 0 else after[c] if dz == 3 else vol[c, dz - 1])[row:row + 1, :].astype(jnp.float32)
            for dz in range(4)
            for c in range(channels)
        ]
        return jnp.concatenate(lines, axis=0).astype(jnp.bfloat16)

    tail[...] = edge(rows - 1)
    head[...] = edge(0)
    down = push(tail, above, sems, 2, (s, jnp.minimum(f + 1, groups - 1)))
    upward = push(head, below, sems, 3, (s, jnp.maximum(f - 1, 0)))
    halo(f, groups, down, upward, above, below)
    for move in moves:
        move.wait()
    turns = []
    for e in range(1, groups):
        peer = lax.rem(f + e, groups)
        turns.append(push(mid.at[pl.ds(peer * parts, parts)], up_out.at[f], (f_send, f_recv), e, (s, peer)))
        turns[-1].start()
    up_out[f] = mid[pl.ds(f * parts, parts)]
    when_sent(f < groups - 1, f > 0, down)
    when_sent(f > 0, f < groups - 1, upward)
    for turn in turns:
        turn.wait()


def deliver(space, groups, pooled, grads, moved, sums, mid, g_mid, g_sum, g_all, f_send, f_recv, z_send, z_recv, gf_send, gf_recv, gz_send, gz_recv):
    s, f = lax.axis_index("space"), lax.axis_index("filt")
    parts = space // groups
    greet(space, groups, s, f)
    turns, g_turns = [], []
    for e in range(1, groups):
        peer = lax.rem(f + e, groups)
        g_turns.append(push(grads.at[peer], g_mid.at[f], (gf_send, gf_recv), e, (s, peer)))
        g_turns[-1].start()
    for e in range(1, groups):
        peer = lax.rem(f + e, groups)
        turns.append(push(pooled.at[peer], mid.at[pl.ds(f * parts, parts)], (f_send, f_recv), e, (s, peer)))
        turns[-1].start()
    g_mid[f] = grads[f]
    mid[pl.ds(f * parts, parts)] = pooled[f]
    for turn in g_turns:
        turn.wait()
    total = g_mid[0]
    for group in range(1, groups):
        total = total + g_mid[group]
    g_sum[...] = total
    g_moves = []
    for d in range(1, space):
        peer = lax.rem(s + d, space)
        g_moves.append(push(g_sum, g_all.at[s], (gz_send, gz_recv), d, (peer, f)))
        g_moves[-1].start()
    g_all[s] = total
    for turn in turns:
        turn.wait()
    moves = []
    for d in range(1, space):
        peer = lax.rem(s + d, space)
        moves.append(push(mid.at[peer], moved.at[s], (z_send, z_recv), d, (peer, f)))
        moves[-1].start()
    moved[s] = mid[s]
    for move in g_moves:
        move.wait()
    total = g_all[0]
    for place in range(1, space):
        total = total + g_all[place]
    sums[...] = total
    for move in moves:
        move.wait()


def shards(volume, first_kernel, second_kernel, upstream):
    space, groups = lax.axis_size("space"), lax.axis_size("filt")
    channels, planes, rows, cols = volume.shape
    filters, outputs = first_kernel.shape[0], second_kernel.shape[0]
    group_out, depth_out, band = upstream.shape
    parts = space // groups
    own = filters // groups
    half = cols // 2
    window = 4 * channels
    vmem = pl.BlockSpec(memory_space=pltpu.VMEM)
    half_type = lambda *shape: jax.ShapeDtypeStruct(shape, jnp.bfloat16)
    dma = lambda *counts: [pltpu.SemaphoreType.DMA((count,)) for count in counts for _ in range(2)]

    before, after, above, below, up = pl.pallas_call(
        functools.partial(collect, space, groups),
        out_shape=(
            half_type(channels, rows, cols),
            half_type(channels, rows, cols),
            half_type(window, cols),
            half_type(window, cols),
            half_type(groups, parts, group_out, band),
        ),
        in_specs=[vmem] * 2,
        out_specs=(vmem,) * 5,
        scratch_shapes=[
            pltpu.VMEM((space, group_out, band), jnp.bfloat16),
            pltpu.VMEM((window, cols), jnp.bfloat16),
            pltpu.VMEM((window, cols), jnp.bfloat16),
            *dma(4, space, groups),
        ],
        compiler_params=pltpu.CompilerParams(collective_id=0, has_side_effects=True, vmem_limit_bytes=32 * 2**20),
        cost_estimate=pl.CostEstimate(flops=10**6, bytes_accessed=10**8, transcendentals=0),
        name="collect",
    )(volume, upstream.transpose(1, 0, 2))

    taps = jnp.pad(first_kernel.reshape(filters, channels * 27), ((0, 0), (0, TAPS - channels * 27)))
    table = jnp.asarray(tap_table(channels), jnp.bfloat16)
    second = second_kernel.transpose(0, 2, 3, 4, 1).reshape(outputs, 8 * filters)
    pooled, grads = pl.pallas_call(
        section,
        out_shape=(
            half_type(groups, parts, group_out, band),
            jax.ShapeDtypeStruct((groups, 9, own, TAPS), jnp.float32),
        ),
        in_specs=[vmem] * 9,
        out_specs=(vmem, vmem),
        scratch_shapes=[
            pltpu.VMEM((4 * half // 128, window * (rows + 2), 128), jnp.float32),
            pltpu.VMEM((8 * filters, 16 * window), jnp.bfloat16),
            pltpu.VMEM((8 * filters, outputs), jnp.bfloat16),
            pltpu.VMEM((8 * filters, 16 * window), jnp.float32),
            pltpu.VMEM((8 * filters, outputs), jnp.float32),
        ],
        compiler_params=pltpu.CompilerParams(vmem_limit_bytes=48 * 2**20),
        cost_estimate=pl.CostEstimate(flops=6 * 10**9, bytes_accessed=4 * 10**6, transcendentals=0),
        name="section",
    )(volume, before, after, above, below, up, taps, table, second)

    moved, sums = pl.pallas_call(
        functools.partial(deliver, space, groups),
        out_shape=(half_type(space, group_out, band), jax.ShapeDtypeStruct((9, own, TAPS), jnp.float32)),
        in_specs=[vmem] * 2,
        out_specs=(vmem, vmem),
        scratch_shapes=[
            pltpu.VMEM((space, group_out, band), jnp.bfloat16),
            pltpu.VMEM((groups, 9, own, TAPS), jnp.float32),
            pltpu.VMEM((9, own, TAPS), jnp.float32),
            pltpu.VMEM((space, 9, own, TAPS), jnp.float32),
            *dma(groups, space, groups, space),
        ],
        compiler_params=pltpu.CompilerParams(collective_id=1, has_side_effects=True, vmem_limit_bytes=32 * 2**20),
        cost_estimate=pl.CostEstimate(flops=10**6, bytes_accessed=10**8, transcendentals=0),
        name="deliver",
    )(pooled, grads)
    grad_first = sums[8, :, 0:channels * 27].reshape(own, channels, 3, 3, 3)
    grad_second = sums[0:8, :, 0:outputs].transpose(2, 1, 0).reshape(outputs, own, 2, 2, 2)
    return (moved.transpose(1, 0, 2), grad_first, grad_second)


def solution(mesh):
    in_specs = (P(None, "space", "filt", None), P(), P(), P("filt", None, "space"))
    out_specs = (
        P("filt", None, "space"),
        P("filt", None, None, None, None),
        P(None, "filt", None, None, None),
    )
    return jax.shard_map(shards, mesh=mesh, in_specs=in_specs, out_specs=out_specs, check_vma=False)
```

time: 240 us -> 106 us (0.44)
  waiting for transfers between devices: 156 us -> 0 us
  Pallas kernels: 13.5 us -> 98.4 us
  starting transfers between devices: 28.7 us -> 0 us
  blocking collectives: 15.2 us -> 0 us
  between operations: 14.3 us -> 0.72 us
  local copies, waits for them, and re-layouts: 9.53 us -> 6.53 us
    psum x1 -> x0, waiting for transfers between devices: 131 us -> none  [shards(): grads = lax.psum(grads, ('space', 'filt'))]
    pallas_call x1 -> x3, Pallas kernels: 13.5 us -> 98.4 us  [the longest x1 42.7 us: shards(): pl.pallas_call(functools.partial(collect, space, groups), out_shape=(half...]
    all_to_all x3 -> x0, starting transfers between devices: 18.2 us -> none  [the longest x1 8.87 us: shards(): moved = lax.all_to_all(moved, 'space', 0, 0, tiled=True)]
    all_to_all x3 -> x0, waiting for transfers between devices: 17.7 us -> none  [the longest x1 17.7 us: shards(): lax.all_to_all(sent, 'space', 0, 0, tiled=True)]
    all_to_all x1 -> x0, blocking collectives: 15.2 us -> none  [shards(): lax.all_to_all(moved, 'filt', 0, 0, tiled=True)]
    ppermute x4 -> x0, starting transfers between devices: 10.5 us -> none  [the longest x1 3.99 us: shards(): lax.ppermute(edges(rows - 1), 'filt', [(i, i + 1) for i in range(ends)])]
    ppermute x4 -> x0, waiting for transfers between devices: 6.91 us -> none  [the longest x1 5.97 us: shards(): lax.ppermute(edges(0), 'filt', [(i + 1, i) for i in range(ends)])]
    unnamed x15 -> x11, local copies, waits for them, and re-layouts: 7.25 us -> 6.17 us
  transfers between devices with their start and end apart: 8 -> 0, of which waited for: 4 -> 0; matrix products, arithmetic and copies ran while one was open for 1% -> 0% of each run, Pallas kernels for 0% -> 0%
where the time goes in v2:
time: 106 us
  Pallas kernels  98.4 us (93%)
  local copies, waits for them, and re-layouts  6.53 us (6%)
    pallas_call x1, Pallas kernels, shards(): pl.pallas_call(functools.partial(collect, space, groups), out_shape=(half...  42.7 us
    pallas_call x1, Pallas kernels, shards(): pl.pallas_call(functools.partial(deliver, space, groups), out_shape=(half...  41.5 us
    pallas_call x1, Pallas kernels, shards(): pl.pallas_call(section, out_shape=(half_type(groups, parts, group_out, ba...  14.2 us
    unnamed x11, local copies, waits for them, and re-layouts  6.17 us

profile of v2, /device:TPU:9, one launch (start us, length us, event | category | flops | bytes accessed | tf_op | source)
XLA Modules:
  0.0 105.7 jit_solution(15341938701520939881)
XLA Ops:
  0.6 0.8 copy.15
  1.4 0.0 copy-start.2
  1.4 0.1 copy.16
  1.5 0.7 copy-done.2
  2.3 0.1 copy.18.second
  2.4 0.0 copy-start
  2.4 1.9 %copy.24 = bf16[16,8,4096]{2,0,1:T(8,128)(2,1)S(1)} copy(bf16[16,8,4096]{2,1,0:T(8,128)(2,1)} %param.8) | data formatting | bytes 2097152 | tf_op args[3]
  4.2 0.0 copy-done
  4.2 0.0 copy-start.1
  4.3 42.7 %collect.1 = (bf16[4,64,512]{2,1,0:T(8,128)(2,1)S(1)}, bf16[4,64,512]{2,1,0:T(8,128)(2,1)S(1)}, bf16[16,512]{1,0:T(8,128)(2,1)S(1)}, bf16[16,512]{1,0:T(8,128)(2,1)S(1)}, bf16[4,2,16,4096]{3,2,1,0:T(8,128)(2,1)S(1)}) custom-call(bf16[4,2,64,512]{3,2,1,0:T(8,128)(2,1)S(1)} %copy-done, bf16[8,16,4096]{2,1,0:T(8,128)(2,1)S(1)} %bitcast.13), custom_call_target="tpu_custom_call" | custom-call | flops 1000000 | bytes 100000000 | tf_op jit(solution)/shard_map/collect/pallas_call | solution.py:250
  47.0 0.0 copy-done.1
  47.0 14.2 %section.1 = (bf16[4,2,16,4096]{3,2,1,0:T(8,128)(2,1)S(1)}, f32[4,9,8,128]{3,2,1,0:T(8,128)S(1)}) custom-call(bf16[4,2,64,512]{3,2,1,0:T(8,128)(2,1)S(1)} %copy-done, bf16[4,64,512]{2,1,0:T(8,128)(2,1)S(1)} %get-tuple-element.12.before, bf16[4,64,512]{2,1,0:T(8,128)(2,1)S(1)} %get-tuple-element.13.after, bf16[16,512]{1,0:T(8,128)(2,1)S(1)} %get-tuple-element.14.above, ...), custom_call_target="tpu_custom_call" | custom-call | flops 6000000000 | bytes 4000000 | tf_op jit(solution)/shard_map/section/pallas_call | solution.py:275
  61.2 41.5 %deliver.1 = (bf16[8,16,4096]{2,1,0:T(8,128)(2,1)S(1)}, f32[9,8,128]{2,1,0:T(8,128)S(1)}) custom-call(bf16[4,2,16,4096]{3,2,1,0:T(8,128)(2,1)S(1)} %get-tuple-element.17.pooled, f32[4,9,8,128]{3,2,1,0:T(8,128)S(1)} %get-tuple-element.18.grads), custom_call_target="tpu_custom_call" | custom-call | flops 1000000 | bytes 100000000 | tf_op jit(solution)/shard_map/deliver/pallas_call | solution.py:295
  102.7 1.6 %copy.20 = bf16[16,8,4096]{2,1,0:T(8,128)(2,1)} copy(bf16[16,8,4096]{2,0,1:T(8,128)(2,1)S(1)} %bitcast.14) | data formatting | bytes 2097152
  104.3 0.6 copy.22
  104.9 0.1 copy.19
  105.0 0.6 copy.21
  (6 shorter events, 0.1 us)
Async XLA Ops:
  1.4 0.8 copy-start.2
  2.4 1.9 %copy-start = (bf16[4,2,64,512]{3,2,1,0:T(8,128)(2,1)S(1)}, bf16[4,2,64,512]{3,2,1,0:T(8,128)(2,1)}, u32[]{:S(2)}) copy-start(bf16[4,2,64,512]{3,2,1,0:T(8,128)(2,1)} %vol.3) | copy-start | bytes 1572868
  4.2 42.7 %copy-start.1 = (bf16[128,2048]{1,0:T(8,128)(2,1)S(1)}, bf16[128,2048]{1,0:T(8,128)(2,1)}, u32[]{:S(2)}) copy-start(bf16[128,2048]{1,0:T(8,128)(2,1)} %constant.5.clone.table) | copy-start | bytes 1572868

commit v3 on v2

v3 whole, which is shorter than its diff:
```python
import functools

import jax
import jax.numpy as jnp
import numpy as np
from jax import lax
from jax.experimental import pallas as pl
from jax.experimental.pallas import tpu as pltpu
from jax.sharding import PartitionSpec as P

SLOPE = 0.3
GROUP = 4
CHUNKS = 2
TAPS = 128
MESH = pl.DeviceIdType.MESH


def tap_table(channels):
    table = np.zeros((TAPS, 8, 4, 4, 4, channels), np.float32)
    for cell in range(8):
        a, b, g = cell // 4, (cell // 2) % 2, cell % 2
        for tap in range(channels * 27):
            c, i, j, k = tap // 27, (tap // 9) % 3, (tap // 3) % 3, tap % 3
            table[tap, cell, g + k, b + j, a + i, c] = 1.0
    return table.reshape(TAPS, 8 * 64 * channels)


def dot(left, right, dims=((1,), (0,)), precision=None):
    return lax.dot_general(left, right, (dims, ((), ())), precision=precision, preferred_element_type=jnp.float32)


def greet(barrier, space, groups, s, f):
    for d in range(1, space):
        pl.semaphore_signal(barrier, inc=1, device_id=(lax.rem(s + d, space), f), device_id_type=MESH)
    for e in range(1, groups):
        pl.semaphore_signal(barrier, inc=1, device_id=(s, lax.rem(f + e, groups)), device_id_type=MESH)


def push(source, target, sems, index, device):
    send, recv = sems
    return pltpu.make_async_remote_copy(
        src_ref=source, dst_ref=target, send_sem=send.at[index], recv_sem=recv.at[index], device_id=device, device_id_type=MESH
    )


def when_sent(there, here, copy):
    @pl.when(there)
    def _():
        copy.wait_send()

    @pl.when(here)
    def _():
        copy.wait_recv()


def halo(s, count, ahead, back, filled, emptied):
    @pl.when(s < count - 1)
    def _():
        ahead.start()

    @pl.when(s > 0)
    def _():
        back.start()

    @pl.when(s == 0)
    def _():
        filled[...] = jnp.zeros_like(filled)

    @pl.when(s == count - 1)
    def _():
        emptied[...] = jnp.zeros_like(emptied)


def section(
    space, groups, vol, up, taps, table, second, moved, sums,
    before, after, above, below, tail, head, up_mid, up_here, pooled, pool_mid,
    cells, first_mat, back_mat, windows, actives, g_first, g_second, grads, g_mid, g_sum, g_all,
    h_send, h_recv, uz_send, uz_recv, uf_send, uf_recv, pf_send, pf_recv, pz_send, pz_recv, gf_send, gf_recv, gz_send, gz_recv,
):
    s, f = lax.axis_index("space"), lax.axis_index("filt")
    channels, planes, rows, cols = vol.shape
    parts = space // groups
    window = channels * 4
    half = cols // 2
    lanes = half // 128
    filters, outputs = taps.shape[0], second.shape[0]
    own = filters // groups
    group_out, band = up.shape[1:]
    size = 16 * window
    width = GROUP * half
    per_part = band // width
    per_chunk = per_part // CHUNKS
    barrier = pltpu.get_barrier_semaphore()
    greet(barrier, space, groups, s, f)
    for cell in range(8):
        first_mat[cell * filters:(cell + 1) * filters, :] = dot(taps[...], table[:, cell * size:(cell + 1) * size]).astype(jnp.bfloat16)
    back_mat[...] = second[...].astype(jnp.float32).T.astype(jnp.bfloat16)
    g_first[...] = jnp.zeros_like(g_first)
    g_second[...] = jnp.zeros_like(g_second)
    pl.semaphore_wait(barrier, space + groups - 2)

    sems = (h_send, h_recv)
    ahead = push(vol.at[:, planes - 1], before, sems, 0, (jnp.minimum(s + 1, space - 1), f))
    back = push(vol.at[:, 0], after, sems, 1, (jnp.maximum(s - 1, 0), f))
    halo(s, space, ahead, back, before, after)
    up_moves = [[] for _ in range(CHUNKS)]
    for k in range(CHUNKS):
        chunk = pl.ds(k * per_chunk * width, per_chunk * width)
        for d in range(1, space):
            peer = lax.rem(s + d, space)
            up_moves[k].append(push(up.at[peer, :, chunk], up_mid.at[s, :, chunk], (uz_send, uz_recv), k * space + d, (peer, f)))
            up_moves[k][-1].start()
    up_mid[s] = up[s]

    source = lax.broadcasted_iota(jnp.int32, (cols, 4 * half), 0)
    target = lax.broadcasted_iota(jnp.int32, (cols, 4 * half), 1)
    pick = (source == 2 * lax.rem(target, half) + lax.div(target, half) - 1).astype(jnp.float32).astype(jnp.bfloat16)

    def fill(dz):
        for c in range(channels):
            plane = before[c] if dz == 0 else after[c] if dz == 3 else vol[c, dz - 1]
            spread = dot(plane, pick)
            for lane in range(4 * lanes):
                cells[lane, pl.ds(window + dz * channels + c, rows, stride=window), :] = spread[:, lane * 128:(lane + 1) * 128]

    fill(1)
    when_sent(s < space - 1, s > 0, ahead)
    when_sent(s > 0, s < space - 1, back)

    def edge(row):
        lines = [
            (before[c] if dz == 0 else after[c] if dz == 3 else vol[c, dz - 1])[row:row + 1, :].astype(jnp.float32)
            for dz in range(4)
            for c in range(channels)
        ]
        return jnp.concatenate(lines, axis=0).astype(jnp.bfloat16)

    tail[...] = edge(rows - 1)
    head[...] = edge(0)
    down = push(tail, above, sems, 2, (s, jnp.minimum(f + 1, groups - 1)))
    upward = push(head, below, sems, 3, (s, jnp.maximum(f - 1, 0)))
    halo(f, groups, down, upward, above, below)
    fill(0)
    fill(2)
    fill(3)
    when_sent(f < groups - 1, f > 0, down)
    when_sent(f > 0, f < groups - 1, upward)
    for border, at in ((above, 0), (below, window * (rows + 1))):
        spread = dot(border[...], pick)
        for lane in range(4 * lanes):
            cells[lane, at:at + window, :] = spread[:, lane * 128:(lane + 1) * 128]

    pool_turns = []
    for part in range(parts):

        def forward(index, carry):
            place = part * per_part + index
            columns = []
            for y in range(GROUP):
                start = pl.multiple_of((place * GROUP + y) * 2 * window, 2 * window)
                tiles = [
                    jnp.concatenate(
                        [cells[dx * lanes + lane, pl.ds(start, 4 * window), :].astype(jnp.bfloat16) for lane in range(lanes)], axis=1
                    )
                    for dx in range(4)
                ]
                columns.append(jnp.concatenate(tiles, axis=0))
            patches = jnp.concatenate(columns, axis=1)
            windows[place] = patches
            first_out = dot(first_mat[...], patches)
            active = jnp.where(first_out > 0, first_out, SLOPE * first_out).astype(jnp.bfloat16)
            actives[place] = active
            pooled_tile = dot(second[...], active).astype(jnp.bfloat16)
            span = pl.ds(pl.multiple_of(index * width, width), width)
            for group in range(groups):
                pooled[group, part, :, span] = pooled_tile[group * group_out:(group + 1) * group_out]
            return carry

        lax.fori_loop(0, per_part, forward, 0)
        for e in range(1, groups):
            peer = lax.rem(f + e, groups)
            pool_turns.append(push(pooled.at[peer, part], pool_mid.at[f * parts + part], (pf_send, pf_recv), part * groups + e, (s, peer)))
            pool_turns[-1].start()
        pool_mid[f * parts + part] = pooled[f, part]

    def backward(index, k):
        part = index // per_chunk
        inner = k * per_chunk + index % per_chunk
        place = part * per_part + inner
        span = pl.ds(pl.multiple_of(inner * width, width), width)
        active = actives[place]
        gradient = jnp.concatenate([up_here[group, part, :, span] for group in range(groups)], axis=0)
        back_flow = dot(back_mat[...], gradient)
        steered = (back_flow * jnp.where(active.astype(jnp.float32) > 0, 1.0, SLOPE)).astype(jnp.bfloat16)
        g_second[...] += dot(active, gradient, ((1,), (1,)))
        g_first[...] += dot(steered, windows[place], ((1,), (1,)))
        return k

    pool_moves = []
    for k in range(CHUNKS):
        chunk = pl.ds(k * per_chunk * width, per_chunk * width)
        for move in up_moves[k]:
            move.wait()
        up_turns = []
        for e in range(1, groups):
            peer = lax.rem(f + e, groups)
            up_turns.append(
                push(up_mid.at[pl.ds(peer * parts, parts), :, chunk], up_here.at[f, :, :, chunk], (uf_send, uf_recv), k * groups + e, (s, peer))
            )
            up_turns[-1].start()
        up_here[f, :, :, chunk] = up_mid[pl.ds(f * parts, parts), :, chunk]
        if k == CHUNKS - 1:
            for turn in pool_turns:
                turn.wait()
            for d in range(1, space):
                peer = lax.rem(s + d, space)
                pool_moves.append(push(pool_mid.at[peer], moved.at[s], (pz_send, pz_recv), d, (peer, f)))
                pool_moves[-1].start()
            moved[s] = pool_mid[s]
        for turn in up_turns:
            turn.wait()
        lax.fori_loop(0, parts * per_chunk, lambda index, carry, k=k: (backward(index, k), carry)[1], 0)

    grads[...] = jnp.zeros_like(grads)
    total = jnp.zeros((filters, TAPS), jnp.float32)
    for cell in range(8):
        piece = table[:, cell * size:(cell + 1) * size].astype(jnp.float32)
        total += dot(g_first[cell * filters:(cell + 1) * filters, :], piece, ((1,), (1,)), lax.Precision.HIGHEST)
    for group in range(groups):
        for cell in range(8):
            first = cell * filters + group * own
            grads[group, cell, :, 0:outputs] = g_second[first:first + own, :]
        grads[group, 8, :, :] = total[group * own:(group + 1) * own]
    g_turns = []
    for e in range(1, groups):
        peer = lax.rem(f + e, groups)
        g_turns.append(push(grads.at[peer], g_mid.at[f], (gf_send, gf_recv), e, (s, peer)))
        g_turns[-1].start()
    g_mid[f] = grads[f]
    for turn in g_turns:
        turn.wait()
    total = g_mid[0]
    for group in range(1, groups):
        total = total + g_mid[group]
    g_sum[...] = total
    g_moves = []
    for d in range(1, space):
        peer = lax.rem(s + d, space)
        g_moves.append(push(g_sum, g_all.at[s], (gz_send, gz_recv), d, (peer, f)))
        g_moves[-1].start()
    g_all[s] = total
    for move in g_moves:
        move.wait()
    total = g_all[0]
    for place in range(1, space):
        total = total + g_all[place]
    sums[...] = total
    for move in pool_moves:
        move.wait()


def shards(volume, first_kernel, second_kernel, upstream):
    space, groups = lax.axis_size("space"), lax.axis_size("filt")
    channels, planes, rows, cols = volume.shape
    filters, outputs = first_kernel.shape[0], second_kernel.shape[0]
    group_out, depth_out, band = upstream.shape
    parts = space // groups
    own = filters // groups
    half = cols // 2
    window = 4 * channels
    vmem = pl.BlockSpec(memory_space=pltpu.VMEM)
    half_type = lambda *shape: jax.ShapeDtypeStruct(shape, jnp.bfloat16)
    dma = lambda *counts: [pltpu.SemaphoreType.DMA((count,)) for count in counts for _ in range(2)]

    taps = jnp.pad(first_kernel.reshape(filters, channels * 27), ((0, 0), (0, TAPS - channels * 27)))
    table = jnp.asarray(tap_table(channels), jnp.bfloat16)
    second = second_kernel.transpose(0, 2, 3, 4, 1).reshape(outputs, 8 * filters)
    depth = 8 * filters
    steps = rows // 2 // GROUP
    bf16 = lambda *shape: pltpu.VMEM(shape, jnp.bfloat16)
    f32 = lambda *shape: pltpu.VMEM(shape, jnp.float32)
    moved, sums = pl.pallas_call(
        functools.partial(section, space, groups),
        out_shape=(half_type(space, group_out, band), jax.ShapeDtypeStruct((9, own, TAPS), jnp.float32)),
        in_specs=[vmem] * 5,
        out_specs=(vmem, vmem),
        scratch_shapes=[
            bf16(channels, rows, cols),
            bf16(channels, rows, cols),
            *[bf16(window, cols) for _ in range(4)],
            bf16(space, group_out, band),
            bf16(groups, parts, group_out, band),
            bf16(groups, parts, group_out, band),
            bf16(space, group_out, band),
            f32(4 * half // 128, window * (rows + 2), 128),
            bf16(depth, 16 * window),
            bf16(depth, outputs),
            bf16(steps, 16 * window, GROUP * half),
            bf16(steps, depth, GROUP * half),
            f32(depth, 16 * window),
            f32(depth, outputs),
            f32(groups, 9, own, TAPS),
            f32(groups, 9, own, TAPS),
            f32(9, own, TAPS),
            f32(space, 9, own, TAPS),
            *dma(4, CHUNKS * space, CHUNKS * groups, parts * groups, space, groups, space),
        ],
        compiler_params=pltpu.CompilerParams(collective_id=0, has_side_effects=True, vmem_limit_bytes=56 * 2**20),
        cost_estimate=pl.CostEstimate(flops=6 * 10**9, bytes_accessed=4 * 10**6, transcendentals=0),
        name="section",
    )(volume, upstream.transpose(1, 0, 2), taps, table, second)
    grad_first = sums[8, :, 0:channels * 27].reshape(own, channels, 3, 3, 3)
    grad_second = sums[0:8, :, 0:outputs].transpose(2, 1, 0).reshape(outputs, own, 2, 2, 2)
    return (moved.transpose(1, 0, 2), grad_first, grad_second)


def solution(mesh):
    in_specs = (P(None, "space", "filt", None), P(), P(), P("filt", None, "space"))
    out_specs = (
        P("filt", None, "space"),
        P("filt", None, None, None, None),
        P(None, "filt", None, None, None),
    )
    return jax.shard_map(shards, mesh=mesh, in_specs=in_specs, out_specs=out_specs, check_vma=False)
```

time: 106 us -> 80.3 us (0.76)
  Pallas kernels: 98.4 us -> 69.4 us
  local copies, waits for them, and re-layouts: 6.53 us -> 9.29 us
    pallas_call x3 -> x1, Pallas kernels: 98.4 us -> 69.4 us  [shards(): pl.pallas_call(functools.partial(section, space, groups), out_shape=(half...]
    unnamed x11 -> x9, local copies, waits for them, and re-layouts: 6.17 us -> 7.7 us
where the time goes in v3:
time: 80.3 us; the launch traced here: 79.4 us
  Pallas kernels  69.4 us (86%)
  local copies, waits for them, and re-layouts  9.29 us (12%)
    pallas_call x1, Pallas kernels, shards(): pl.pallas_call(functools.partial(section, space, groups), out_shape=(half...  69.4 us
    unnamed x9, local copies, waits for them, and re-layouts  7.7 us

profile of v3, /device:TPU:9, one launch (start us, length us, event | category | flops | bytes accessed | tf_op | source)
XLA Modules:
  0.0 79.4 jit_solution(1492101162749663103)
XLA Ops:
  0.6 0.8 copy.15
  1.4 0.0 copy-start
  1.4 0.1 copy.16
  1.5 0.6 pad.4.taps
  2.1 0.1 copy-done
  2.3 0.7 copy.18.second
  3.0 2.8 %copy.24 = bf16[16,8,4096]{2,0,1:T(8,128)(2,1)} copy(bf16[16,8,4096]{2,1,0:T(8,128)(2,1)} %param.8) | data formatting | bytes 2097152 | tf_op args[3]
  5.7 69.4 %section.1 = (bf16[8,16,4096]{2,1,0:T(8,128)(2,1)}, f32[9,8,128]{2,1,0:T(8,128)}) custom-call(bf16[4,2,64,512]{3,2,1,0:T(8,128)(2,1)} %vol.1, bf16[8,16,4096]{2,1,0:T(8,128)(2,1)} %bitcast.14, bf16[32,128]{1,0:T(8,128)(2,1)} %pad.4.taps, bf16[128,2048]{1,0:T(8,128)(2,1)} %constant.5.clone.table, bf16[64,256]{1,0:T(8,128)(2,1)} %copy.18.second), custom_call_target="tpu_custom_call" | custom-call | flops 6000000000 | bytes 4000000 | tf_op jit(solution)/shard_map/section/pallas_call | solution.py:282
  75.2 0.0 copy-start.1
  75.2 2.8 %copy.20 = bf16[16,8,4096]{2,1,0:T(8,128)(2,1)} copy(bf16[16,8,4096]{2,0,1:T(8,128)(2,1)} %bitcast.13) | data formatting | bytes 2097152
  78.0 0.0 copy-done.1
  78.0 0.6 copy.22
  78.6 0.1 copy.19
  78.8 0.6 copy.21
  (5 shorter events, 0.1 us)
Async XLA Ops:
  1.4 0.8 %copy-start = (bf16[64,32,2,2,2]{0,4,3,2,1:T(2,128)(2,1)S(1)}, bf16[64,32,2,2,2]{0,4,3,2,1:T(2,128)(2,1)}, u32[]{:S(2)}) copy-start(bf16[64,32,2,2,2]{0,4,3,2,1:T(2,128)(2,1)} %param.7) | copy-start | bytes 98308
  75.2 2.8 %copy-start.1 = (f32[9,8,128]{2,1,0:T(8,128)S(1)}, f32[9,8,128]{2,1,0:T(8,128)}, u32[]{:S(2)}) copy-start(f32[9,8,128]{2,1,0:T(8,128)} %get-tuple-element.6) | copy-start | bytes 110596

commit v4 on v3

--- a/solution.py
+++ b/solution.py
@@ -103,10 +103,11 @@
     ahead = push(vol.at[:, planes - 1], before, sems, 0, (jnp.minimum(s + 1, space - 1), f))
     back = push(vol.at[:, 0], after, sems, 1, (jnp.maximum(s - 1, 0), f))
     halo(s, space, ahead, back, before, after)
+    far_first = sorted(range(1, space), key=lambda d: (abs(2 * d - space), d))
     up_moves = [[] for _ in range(CHUNKS)]
     for k in range(CHUNKS):
         chunk = pl.ds(k * per_chunk * width, per_chunk * width)
-        for d in range(1, space):
+        for d in far_first:
             peer = lax.rem(s + d, space)
             up_moves[k].append(push(up.at[peer, :, chunk], up_mid.at[s, :, chunk], (uz_send, uz_recv), k * space + d, (peer, f)))
             up_moves[k][-1].start()
@@ -197,6 +198,13 @@
         return k
 
     pool_moves = []
+
+    def pool_start(until):
+        for d in far_first[len(pool_moves):until]:
+            peer = lax.rem(s + d, space)
+            pool_moves.append(push(pool_mid.at[peer], moved.at[s], (pz_send, pz_recv), d, (peer, f)))
+            pool_moves[-1].start()
+
     for k in range(CHUNKS):
         chunk = pl.ds(k * per_chunk * width, per_chunk * width)
         for move in up_moves[k]:
@@ -209,14 +217,10 @@
             )
             up_turns[-1].start()
         up_here[f, :, :, chunk] = up_mid[pl.ds(f * parts, parts), :, chunk]
-        if k == CHUNKS - 1:
+        if k == 0:
             for turn in pool_turns:
                 turn.wait()
-            for d in range(1, space):
-                peer = lax.rem(s + d, space)
-                pool_moves.append(push(pool_mid.at[peer], moved.at[s], (pz_send, pz_recv), d, (peer, f)))
-                pool_moves[-1].start()
-            moved[s] = pool_mid[s]
+        pool_start((k + 1) * space // (2 * CHUNKS))
         for turn in up_turns:
             turn.wait()
         lax.fori_loop(0, parts * per_chunk, lambda index, carry, k=k: (backward(index, k), carry)[1], 0)
@@ -236,6 +240,7 @@
         peer = lax.rem(f + e, groups)
         g_turns.append(push(grads.at[peer], g_mid.at[f], (gf_send, gf_recv), e, (s, peer)))
         g_turns[-1].start()
+    pool_start(5 * space // 8)
     g_mid[f] = grads[f]
     for turn in g_turns:
         turn.wait()
@@ -248,6 +253,8 @@
         peer = lax.rem(s + d, space)
         g_moves.append(push(g_sum, g_all.at[s], (gz_send, gz_recv), d, (peer, f)))
         g_moves[-1].start()
+    pool_start(space)
+    moved[s] = pool_mid[s]
     g_all[s] = total
     for move in g_moves:
         move.wait()

time: 80.3 us -> 77.1 us (0.960)
  Pallas kernels: 69.4 us -> 65.8 us
    pallas_call x1, Pallas kernels: 69.4 us -> 65.8 us  [shards(): pl.pallas_call(functools.partial(section, space, groups), out_shape=(half...]
where the time goes in v4:
time: 77.1 us; the launch traced here: 75.8 us
  Pallas kernels  65.8 us (85%)
  local copies, waits for them, and re-layouts  9.29 us (12%)
    pallas_call x1, Pallas kernels, shards(): pl.pallas_call(functools.partial(section, space, groups), out_shape=(half...  65.8 us
    unnamed x9, local copies, waits for them, and re-layouts  7.7 us

profile of v4, /device:TPU:9, one launch (start us, length us, event | category | flops | bytes accessed | tf_op | source)
XLA Modules:
  0.0 75.8 jit_solution(1917212127603531742)
XLA Ops:
  0.6 0.8 %copy.15 = bf16[32,4,3,3,3]{0,4,3,2,1:T(4,128)(2,1)S(1)} copy(bf16[32,4,3,3,3]{0,1,4,3,2:T(4,128)(2,1)} %param.6) | data formatting | bytes 13824 | tf_op args[1]
  1.4 0.0 copy-start
  1.4 0.1 copy.16
  1.5 0.6 pad.4.taps
  2.1 0.1 copy-done
  2.3 0.7 copy.18.second
  3.0 2.8 %copy.24 = bf16[16,8,4096]{2,0,1:T(8,128)(2,1)} copy(bf16[16,8,4096]{2,1,0:T(8,128)(2,1)} %param.8) | data formatting | bytes 2097152 | tf_op args[3]
  5.7 65.8 %section.1 = (bf16[8,16,4096]{2,1,0:T(8,128)(2,1)}, f32[9,8,128]{2,1,0:T(8,128)}) custom-call(bf16[4,2,64,512]{3,2,1,0:T(8,128)(2,1)} %vol.1, bf16[8,16,4096]{2,1,0:T(8,128)(2,1)} %bitcast.14, bf16[32,128]{1,0:T(8,128)(2,1)} %pad.4.taps, bf16[128,2048]{1,0:T(8,128)(2,1)} %constant.5.clone.table, bf16[64,256]{1,0:T(8,128)(2,1)} %copy.18.second), custom_call_target="tpu_custom_call" | custom-call | flops 6000000000 | bytes 4000000 | tf_op jit(solution)/shard_map/section/pallas_call | solution.py:289
  71.5 0.0 copy-start.1
  71.6 2.8 %copy.20 = bf16[16,8,4096]{2,1,0:T(8,128)(2,1)} copy(bf16[16,8,4096]{2,0,1:T(8,128)(2,1)} %bitcast.13) | data formatting | bytes 2097152
  74.3 0.0 copy-done.1
  74.3 0.6 copy.22
  75.0 0.1 copy.19
  75.1 0.6 copy.21
  (5 shorter events, 0.1 us)
Async XLA Ops:
  1.4 0.8 %copy-start = (bf16[64,32,2,2,2]{0,4,3,2,1:T(2,128)(2,1)S(1)}, bf16[64,32,2,2,2]{0,4,3,2,1:T(2,128)(2,1)}, u32[]{:S(2)}) copy-start(bf16[64,32,2,2,2]{0,4,3,2,1:T(2,128)(2,1)} %param.7) | copy-start | bytes 98308
  71.5 2.8 %copy-start.1 = (f32[9,8,128]{2,1,0:T(8,128)S(1)}, f32[9,8,128]{2,1,0:T(8,128)}, u32[]{:S(2)}) copy-start(f32[9,8,128]{2,1,0:T(8,128)} %get-tuple-element.6) | copy-start | bytes 110596

commit v5 on v4

--- a/solution.py
+++ b/solution.py
@@ -220,7 +220,7 @@
         if k == 0:
             for turn in pool_turns:
                 turn.wait()
-        pool_start((k + 1) * space // (2 * CHUNKS))
+        pool_start(3 * (k + 1) * space // (4 * CHUNKS))
         for turn in up_turns:
             turn.wait()
         lax.fori_loop(0, parts * per_chunk, lambda index, carry, k=k: (backward(index, k), carry)[1], 0)
@@ -240,7 +240,6 @@
         peer = lax.rem(f + e, groups)
         g_turns.append(push(grads.at[peer], g_mid.at[f], (gf_send, gf_recv), e, (s, peer)))
         g_turns[-1].start()
-    pool_start(5 * space // 8)
     g_mid[f] = grads[f]
     for turn in g_turns:
         turn.wait()

time: 77.1 us -> 78.8 us (1.022)
  the two profiles are of different devices: /device:TPU:9 before, /device:TPU:1 now
where the time goes in v5:
time: 78.8 us; the launch traced here: 78.5 us
  Pallas kernels  68.5 us (87%)
  local copies, waits for them, and re-layouts  9.29 us (12%)
    pallas_call x1, Pallas kernels, shards(): pl.pallas_call(functools.partial(section, space, groups), out_shape=(half...  68.5 us
    unnamed x9, local copies, waits for them, and re-layouts  7.7 us

profile of v5, /device:TPU:1, one launch (start us, length us, event | category | flops | bytes accessed | tf_op | source)
XLA Modules:
  0.0 78.5 jit_solution(4093057306650990837)
XLA Ops:
  0.6 0.8 copy.15
  1.4 0.0 copy-start
  1.4 0.1 copy.16
  1.5 0.6 pad.4.taps
  2.1 0.1 copy-done
  2.3 0.7 copy.18.second
  3.0 2.8 %copy.24 = bf16[16,8,4096]{2,0,1:T(8,128)(2,1)} copy(bf16[16,8,4096]{2,1,0:T(8,128)(2,1)} %param.8) | data formatting | bytes 2097152 | tf_op args[3]
  5.7 68.5 %section.1 = (bf16[8,16,4096]{2,1,0:T(8,128)(2,1)}, f32[9,8,128]{2,1,0:T(8,128)}) custom-call(bf16[4,2,64,512]{3,2,1,0:T(8,128)(2,1)} %vol.1, bf16[8,16,4096]{2,1,0:T(8,128)(2,1)} %bitcast.14, bf16[32,128]{1,0:T(8,128)(2,1)} %pad.4.taps, bf16[128,2048]{1,0:T(8,128)(2,1)} %constant.5.clone.table, bf16[64,256]{1,0:T(8,128)(2,1)} %copy.18.second), custom_call_target="tpu_custom_call" | custom-call | flops 6000000000 | bytes 4000000 | tf_op jit(solution)/shard_map/section/pallas_call | solution.py:288
  74.3 0.0 copy-start.1
  74.3 2.8 %copy.20 = bf16[16,8,4096]{2,1,0:T(8,128)(2,1)} copy(bf16[16,8,4096]{2,0,1:T(8,128)(2,1)} %bitcast.13) | data formatting | bytes 2097152
  77.1 0.0 copy-done.1
  77.1 0.6 copy.22
  77.7 0.1 copy.19
  77.9 0.6 copy.21
  (5 shorter events, 0.1 us)
Async XLA Ops:
  1.4 0.8 %copy-start = (bf16[64,32,2,2,2]{0,4,3,2,1:T(2,128)(2,1)S(1)}, bf16[64,32,2,2,2]{0,4,3,2,1:T(2,128)(2,1)}, u32[]{:S(2)}) copy-start(bf16[64,32,2,2,2]{0,4,3,2,1:T(2,128)(2,1)} %param.7) | copy-start | bytes 98308
  74.3 2.8 %copy-start.1 = (f32[9,8,128]{2,1,0:T(8,128)S(1)}, f32[9,8,128]{2,1,0:T(8,128)}, u32[]{:S(2)}) copy-start(f32[9,8,128]{2,1,0:T(8,128)} %get-tuple-element.6) | copy-start | bytes 110596
